TPU v7x, 32 devices: a whole 2x2x4 slice. The times are simulated.
32 devices in a mesh: dp: 4 (over y, x), fsdp: 8 (over z, core).
Axes of the slice: x: 2, y: 2, z: 4, core: 2. Of those that a mesh axis runs over, the one named last changes fastest.
Arguments:
- tokens: bfloat16 [32, 1024, 768], P(('dp', 'fsdp')), may hold values from -6 to 6
- memory_init: float32 [10, 768], replicated, may hold values from -6 to 6
- chain_tokens: int32 [32], P(('dp', 'fsdp')), may hold values from 128 to 1024, as said below
- cotangent: bfloat16 [32, 1024, 768], P(('dp', 'fsdp')), may hold values from -6 to 6
- weights: float32 [9216, 768], P(('dp', 'fsdp'))
- weight_first: float32 [9216, 768], P(('dp', 'fsdp')), may hold values from -0.6 to 0.6
- weight_second: float32 [9216, 768], P(('dp', 'fsdp')), may hold values from 0.01 to 0.1
- vectors: float32 [12, 768], replicated
- vector_first: float32 [12, 768], replicated, may hold values from -0.6 to 0.6
- vector_second: float32 [12, 768], replicated, may hold values from 0.01 to 0.1
Outputs:
- output: float32 [32, 1024, 768], P(('dp', 'fsdp'))
- token_grad: float32 [32, 1024, 768], P(('dp', 'fsdp'))
- memory_grad: float32 [10, 768], replicated
- weight_grad: float32 [9216, 768], P(('dp', 'fsdp'))
- weight_step: float32 [9216, 768], P(('dp', 'fsdp'))
- new_weight_first: float32 [9216, 768], P(('dp', 'fsdp'))
- new_weight_second: float32 [9216, 768], P(('dp', 'fsdp'))
- vector_grad: float32 [12, 768], replicated
- vector_step: float32 [12, 768], replicated
- new_vector_first: float32 [12, 768], replicated
- new_vector_second: float32 [12, 768], replicated
Inputs may be any that keep to these rules, and one draw needn't show every extreme that they name: `chain_tokens`: each chain's number of true tokens; one chain of every draw has 1024.
All inputs are finite; a program needn't handle non-finite values.
Results may differ from a plain program's by a relative error of at most 0.018.
The roundings to bfloat16 on the way count: a program that leaves them out, or rounds other values in their place, can miss the bound.
Values may be sent and summed in bfloat16 or wider, within the bound.
No kernel may reach another device: no remote copies, remote signals or barrier semaphores. Data moves between devices by JAX's collectives and lax.ppermute only.
A program may use at most 320 MiB of HBM per device.

v0:
```python
import jax
import jax.numpy as jnp
from jax import lax
from jax.sharding import PartitionSpec as P

D = 768
HEADS = 12
FF = 3072
MEM = 10
SEG_LEN = 512
SEGS = 2


eps_norm = 1e-12
beta_one = 0.9
beta_two = 0.95
decay_rate = 0.1
adam_eps = 1e-08
adam_step = 10
neg_large = -1e30


def normalize(values, gain_row, shift_row):
    centred = values - jnp.mean(values, axis=-1, keepdims=True)
    inverse = lax.rsqrt(jnp.mean(centred * centred, axis=-1, keepdims=True) + eps_norm)
    normed = centred * inverse
    return (normed * gain_row + shift_row, normed, inverse)


def norm_back(gradient, normed, inverse, gain_row):
    scaled = gradient * gain_row
    centred = scaled - jnp.mean(scaled, axis=-1, keepdims=True)
    back = inverse * (centred - normed * jnp.mean(scaled * normed, axis=-1, keepdims=True))
    return (back, jnp.sum(gradient * normed, axis=(0, 1)), jnp.sum(gradient, axis=(0, 1)))


def gelu_slope(values):
    return (
        0.5 * (1.0 + lax.erf(values * 0.7071067811865476))
        + values * jnp.exp(-0.5 * values * values) * 0.3989422804014327
    )


def unpack(gathered, model_width, hidden_width):
    stacked = gathered[0 : 3 * model_width].reshape(3, model_width, model_width)
    w_out = gathered[3 * model_width : 4 * model_width]
    w_up = gathered[4 * model_width : 4 * model_width + hidden_width]
    w_down = gathered[4 * model_width + hidden_width :]
    return (stacked, w_out, w_up, w_down)


def score_rows(queries, key_rows, valid_keys):
    head_width = queries.shape[-1]
    scores = jnp.einsum(
        "clhe,cmhe->chlm", queries, key_rows, preferred_element_type=jnp.float32
    ) * head_width ** (-0.5)
    return jnp.where(valid_keys[:, None, None, :], scores, neg_large)


def segment_masks(chain_tokens, segment, chains):
    offset = segment * SEG_LEN
    token_live = jnp.arange(SEG_LEN, dtype=jnp.int32)[None, :] + offset < chain_tokens[:, None]
    segment_real = offset < chain_tokens
    always = jnp.ones((chains, MEM), dtype=jnp.bool_)
    valid_keys = jnp.concatenate([always, token_live, always], axis=1)
    return (token_live, segment_real, valid_keys)


def forward_segment(inputs, valid_keys, matrices, vectors, head_count):
    stacked, w_out, w_up, w_down = matrices
    chains, row_count, model_width = inputs.shape
    head_width = model_width // head_count
    split_shape = (chains, row_count, head_count, head_width)
    lowered = inputs.astype(jnp.bfloat16)
    projected = jnp.einsum("cld,jde->jcle", lowered, stacked, preferred_element_type=jnp.float32)
    queries = (projected[0] + vectors[0]).astype(jnp.bfloat16).reshape(split_shape)
    key_rows = projected[1].astype(jnp.bfloat16).reshape(split_shape)
    value_rows = (projected[2] + vectors[1]).astype(jnp.bfloat16).reshape(split_shape)
    scores = score_rows(queries, key_rows, valid_keys)
    row_max = jnp.max(scores, axis=-1, keepdims=True)
    log_total = row_max + jnp.log(jnp.sum(jnp.exp(scores - row_max), axis=-1, keepdims=True))
    soft_low = jnp.exp(scores - log_total).astype(jnp.bfloat16)
    attended = jnp.einsum(
        "chlm,cmhe->clhe", soft_low, value_rows, preferred_element_type=jnp.float32
    )
    attended = attended.reshape(chains, row_count, model_width).astype(jnp.bfloat16)
    branch = (
        jnp.einsum("cld,de->cle", attended, w_out, preferred_element_type=jnp.float32) + vectors[2]
    )
    after_attention, normed_one, inverse_one = normalize(inputs + branch, vectors[3], vectors[4])
    first_low = after_attention.astype(jnp.bfloat16)
    up_projection = jnp.einsum(
        "cld,fd->clf", first_low, w_up, preferred_element_type=jnp.float32
    ) + vectors[8:].reshape(-1)
    activated = jax.nn.gelu(up_projection, approximate=False).astype(jnp.bfloat16)
    feed_output = (
        jnp.einsum("clf,fd->cld", activated, w_down, preferred_element_type=jnp.float32)
        + vectors[5]
    )
    result, normed_two, inverse_two = normalize(
        after_attention + feed_output, vectors[6], vectors[7]
    )
    saved = (
        lowered,
        queries,
        key_rows,
        value_rows,
        log_total,
        attended,
        normed_one,
        inverse_one,
        first_low,
        up_projection,
        activated,
        normed_two,
        inverse_two,
        valid_keys,
    )
    return (result, saved)


def backward_segment(gradient, saved, matrices, vectors, head_count):
    stacked, w_out, w_up, w_down = matrices
    (
        lowered,
        queries,
        key_rows,
        value_rows,
        log_total,
        attended,
        normed_one,
        inverse_one,
        first_low,
        up_projection,
        activated,
        normed_two,
        inverse_two,
        valid_keys,
    ) = saved
    chains, row_count, model_width = gradient.shape
    head_width = model_width // head_count
    back_two, gain_two, shift_two = norm_back(gradient, normed_two, inverse_two, vectors[6])
    feed_low = back_two.astype(jnp.bfloat16)
    grad_down = jnp.einsum("clf,cld->fd", activated, feed_low, preferred_element_type=jnp.float32)
    bias_down = jnp.sum(feed_low, axis=(0, 1), dtype=jnp.float32)
    acted_grad = jnp.einsum("cld,fd->clf", feed_low, w_down, preferred_element_type=jnp.float32)
    up_low = (acted_grad * gelu_slope(up_projection)).astype(jnp.bfloat16)
    grad_up = jnp.einsum("clf,cld->fd", up_low, first_low, preferred_element_type=jnp.float32)
    bias_up = jnp.sum(up_low, axis=(0, 1), dtype=jnp.float32)
    first_grad = back_two + jnp.einsum(
        "clf,fd->cld", up_low, w_up, preferred_element_type=jnp.float32
    )
    back_one, gain_one, shift_one = norm_back(first_grad, normed_one, inverse_one, vectors[3])
    branch_low = back_one.astype(jnp.bfloat16)
    grad_out = jnp.einsum("cld,cle->de", attended, branch_low, preferred_element_type=jnp.float32)
    bias_out = jnp.sum(branch_low, axis=(0, 1), dtype=jnp.float32)
    attended_grad = jnp.einsum("cle,de->cld", branch_low, w_out, preferred_element_type=jnp.float32)
    attended_grad = attended_grad.astype(jnp.bfloat16).reshape(
        chains, row_count, head_count, head_width
    )
    soft_full = jnp.exp(score_rows(queries, key_rows, valid_keys) - log_total)
    soft_low = soft_full.astype(jnp.bfloat16)
    value_grad = jnp.einsum(
        "chlm,clhe->cmhe", soft_low, attended_grad, preferred_element_type=jnp.float32
    )
    soft_grad = jnp.einsum(
        "clhe,cmhe->chlm", attended_grad, value_rows, preferred_element_type=jnp.float32
    )
    row_inner = jnp.sum(soft_full * soft_grad, axis=-1, keepdims=True)
    score_low = (soft_full * (soft_grad - row_inner)).astype(jnp.bfloat16)
    scale_factor = head_width ** (-0.5)
    query_grad = (
        jnp.einsum("chlm,cmhe->clhe", score_low, key_rows, preferred_element_type=jnp.float32)
        * scale_factor
    )
    key_grad = (
        jnp.einsum("chlm,clhe->cmhe", score_low, queries, preferred_element_type=jnp.float32)
        * scale_factor
    )
    projection_grads = (
        jnp.stack([query_grad, key_grad, value_grad])
        .reshape(3, chains, row_count, model_width)
        .astype(jnp.bfloat16)
    )
    grad_stack = jnp.einsum(
        "cld,jcle->jde", lowered, projection_grads, preferred_element_type=jnp.float32
    )
    bias_triple = jnp.sum(projection_grads, axis=(1, 2), dtype=jnp.float32)
    input_grad = back_one + jnp.einsum(
        "jcle,jde->cld", projection_grads, stacked, preferred_element_type=jnp.float32
    )
    matrix_grad = jnp.concatenate(
        [grad_stack.reshape(3 * model_width, model_width), grad_out, grad_up, grad_down], axis=0
    )
    vector_rows = jnp.stack(
        [
            bias_triple[0],
            bias_triple[2],
            bias_out,
            gain_one,
            shift_one,
            bias_down,
            gain_two,
            shift_two,
        ]
    )
    vector_grad = jnp.concatenate([vector_rows, bias_up.reshape(-1, model_width)], axis=0)
    return (input_grad, matrix_grad, vector_grad)


def adam_update(parameter, gradient, moment_one, moment_two, decay_factor):
    new_one = beta_one * moment_one + (1.0 - beta_one) * gradient
    new_two = beta_two * moment_two + (1.0 - beta_two) * gradient * gradient
    corrected_one = new_one / (1.0 - beta_one**adam_step)
    corrected_two = new_two / (1.0 - beta_two**adam_step)
    update = corrected_one / (jnp.sqrt(corrected_two) + adam_eps) + decay_factor * parameter
    return (update, new_one, new_two)


def shards(
    tokens,
    memory_init,
    chain_tokens,
    cotangent,
    weights,
    weight_first,
    weight_second,
    vectors,
    vector_first,
    vector_second,
):
    chains = tokens.shape[0]
    total_chains = chains * lax.axis_size(("dp", "fsdp"))
    grad_scale = float(total_chains * SEGS * SEG_LEN) ** (-0.5)
    weight_shard = weights.astype(jnp.bfloat16)
    matrices = unpack(lax.all_gather(weight_shard, ("dp", "fsdp"), axis=0, tiled=True), D, FF)
    memory_state = jnp.broadcast_to(memory_init, (chains, MEM, D))
    saved_list = []
    output_rows = []
    for segment in range(SEGS):
        offset = segment * SEG_LEN
        token_live, segment_real, valid_keys = segment_masks(chain_tokens, segment, chains)
        inputs = jnp.concatenate(
            [memory_state, tokens[:, offset : offset + SEG_LEN].astype(jnp.float32), memory_state],
            axis=1,
        )
        result, saved = forward_segment(inputs, valid_keys, matrices, vectors, HEADS)
        saved_list.append(saved)
        output_rows.append(jnp.where(token_live[..., None], result[:, MEM : MEM + SEG_LEN], 0.0))
        written = result[:, MEM + SEG_LEN :]
        memory_state = jnp.where(segment_real[:, None, None], written, memory_state)
    output = jnp.concatenate(output_rows, axis=1)
    back_matrices = unpack(lax.all_gather(weight_shard, ("dp", "fsdp"), axis=0, tiled=True), D, FF)
    carried = jnp.zeros((chains, MEM, D), jnp.float32)
    read_zero = jnp.zeros((chains, MEM, D), jnp.float32)
    matrix_total = jnp.zeros((4 * D + 2 * FF, D), jnp.float32)
    vector_total = jnp.zeros(vectors.shape, jnp.float32)
    token_grads = []
    for segment in range(SEGS - 1, -1, -1):
        offset = segment * SEG_LEN
        token_live, segment_real, valid_keys = segment_masks(chain_tokens, segment, chains)
        token_cot = jnp.where(
            token_live[..., None], cotangent[:, offset : offset + SEG_LEN].astype(jnp.float32), 0.0
        )
        write_cot = jnp.where(segment_real[:, None, None], carried, 0.0)
        gradient = jnp.concatenate([read_zero, token_cot, write_cot], axis=1)
        input_grad, matrix_grad, vector_grad = backward_segment(
            gradient, saved_list[segment], back_matrices, vectors, HEADS
        )
        token_grads.insert(0, input_grad[:, MEM : MEM + SEG_LEN])
        carried = (
            input_grad[:, :MEM]
            + input_grad[:, MEM + SEG_LEN :]
            + jnp.where(segment_real[:, None, None], 0.0, carried)
        )
        matrix_total = matrix_total + matrix_grad
        vector_total = vector_total + vector_grad
    token_grad = jnp.concatenate(token_grads, axis=1)
    memory_local = jnp.sum(carried, axis=0)
    weight_sum = lax.psum_scatter(matrix_total, ("dp", "fsdp"), scatter_dimension=0, tiled=True)
    vector_sum, memory_sum = lax.psum((vector_total, memory_local), ("dp", "fsdp"))
    weight_grad = weight_sum * grad_scale
    vector_grad = vector_sum * grad_scale
    memory_grad = memory_sum * grad_scale
    weight_step, new_weight_first, new_weight_second = adam_update(
        weights, weight_grad, weight_first, weight_second, decay_rate
    )
    vector_step, new_vector_first, new_vector_second = adam_update(
        vectors, vector_grad, vector_first, vector_second, 0.0
    )
    return (
        output,
        token_grad,
        memory_grad,
        weight_grad,
        weight_step,
        new_weight_first,
        new_weight_second,
        vector_grad,
        vector_step,
        new_vector_first,
        new_vector_second,
    )


def solution(mesh):
    return jax.shard_map(
        shards,
        mesh=mesh,
        in_specs=(
            P(("dp", "fsdp"), None, None),
            P(),
            P(("dp", "fsdp")),
            P(("dp", "fsdp"), None, None),
            P(("dp", "fsdp"), None),
            P(("dp", "fsdp"), None),
            P(("dp", "fsdp"), None),
            P(),
            P(),
            P(),
        ),
        out_specs=(
            P(("dp", "fsdp"), None, None),
            P(("dp", "fsdp"), None, None),
            P(),
            P(("dp", "fsdp"), None),
            P(("dp", "fsdp"), None),
            P(("dp", "fsdp"), None),
            P(("dp", "fsdp"), None),
            P(),
            P(),
            P(),
            P(),
        ),
        check_vma=False,
    )
```

profile of v0, /device:TPU:0, one launch (start us, length us, event | category | flops | bytes accessed | tf_op | source)
XLA Modules:
  0.0 851.9 jit_solution(5494647296097375364)
XLA Ops:
  12.6 2.8 bitcast_convert_fusion
  15.4 102.2 %all-gather.2.cloned.1.call-done = bf16[9216,768]{1,0:T(8,128)(2,1)} async-done(((bf16[288,768]{1,0:T(8,128)(2,1)}), bf16[9216,768]{1,0:T(8,128)(2,1)}) %all-gather.2.cloned.1.call-update) | async-done | bytes 14155792 | tf_op jit(solution)/shard_map/all_gather | solution.py:236
  117.6 2.2 slice.163
  127.4 7.9 fusion
  135.3 9.1 %exponential_reduce_fusion.1 = f32[12,532]{1,0:T(8,128)S(1)} fusion(f32[12,532,532]{1,2,0:T(8,128)} %get-tuple-element.72, f32[12,532]{1,0:T(8,128)S(1)} %get-tuple-element.71, pred[532]{0:T(1024)(128)(4,1)S(1)} %get-tuple-element.34), kind=kLoop, calls=%fused_computation.9 | loop fusion | flops 13578768 | bytes 13636756 | tf_op jit(solution)/shard_map/reduce_sum | solution.py:81
  144.5 10.1 %fusion.2 = bf16[12,532,532]{1,2,0:T(8,128)(2,1)} fusion(f32[12,532,532]{1,2,0:T(8,128)} %get-tuple-element.72, f32[12,532]{1,0:T(8,128)S(1)} %log_add_fusion.1, pred[532]{0:T(1024)(128)(4,1)S(1)} %get-tuple-element.34), kind=kLoop, calls=%fused_computation.17 | loop fusion | flops 13585152 | bytes 20403796 | tf_op jit(solution)/shard_map/convert_element_type | solution.py:82
  156.5 5.8 convolution_convert_fusion.3
  162.3 3.5 fusion.130
  166.2 18.4 %fusion.6 = (bf16[532,3072]{1,0:T(8,128)(2,1)S(1)}, f32[532,3072]{1,0:T(8,128)}) fusion(f32[3072]{0:T(1024)S(1)} %add.334, bf16[9216,768]{1,0:T(8,128)(2,1)S(1)} %bitcast.195, f32[532,768]{1,0:T(8,128)S(1)} %get-tuple-element.74, f32[768]{0:T(1024)S(1)} %get-tuple-element.27, f32[768]{0:T(1024)S(1)} %get-tuple-element.28, f32[532]{0:T(1024)S(1)} %add_rsqrt_fusion.3, ...), kind=kOutput, calls=%fused_computation.21 | convolution fusion | flops 2620197888 | bytes 16199680 | tf_op jit(solution)/shard_map/cld,fd->clf/dot_general | solution.py:92
  184.7 2.9 fusion.131
  196.1 2.2 copy.52
  198.3 7.9 fusion.1
  206.2 9.1 %exponential_reduce_fusion = f32[12,532]{1,0:T(8,128)S(1)} fusion(f32[12,532,532]{1,2,0:T(8,128)} %get-tuple-element.80, f32[12,532]{1,0:T(8,128)S(1)} %get-tuple-element.79, pred[532]{0:T(1024)(128)(4,1)S(1)} %get-tuple-element.33), kind=kLoop, calls=%fused_computation.6 | loop fusion | flops 13578768 | bytes 13636756 | tf_op jit(solution)/shard_map/reduce_sum | solution.py:81
  215.4 10.4 %fusion.3 = bf16[12,532,532]{1,2,0:T(8,128)(2,1)} fusion(f32[12,532,532]{1,2,0:T(8,128)} %get-tuple-element.80, f32[12,532]{1,0:T(8,128)S(1)} %log_add_fusion, pred[532]{0:T(1024)(128)(4,1)S(1)} %get-tuple-element.33), kind=kLoop, calls=%fused_computation.18 | loop fusion | flops 13585152 | bytes 20403796 | tf_op jit(solution)/shard_map/convert_element_type | solution.py:82
  227.7 5.2 convolution_convert_fusion.2
  233.0 3.4 fusion.132
  236.9 18.2 %fusion.9 = (bf16[532,3072]{1,0:T(8,128)(2,1)S(1)}, f32[532,3072]{1,0:T(8,128)}) fusion(f32[3072]{0:T(1024)S(1)} %add.334, bf16[9216,768]{1,0:T(8,128)(2,1)S(1)} %bitcast.197, f32[532,768]{1,0:T(8,128)S(1)} %get-tuple-element.82, f32[532]{0:T(1024)S(1)} %add_rsqrt_fusion.1, f32[532]{0:T(1024)S(1)} %broadcast_multiply_fusion.12, ...), kind=kOutput, calls=%fused_computation.24 | convolution fusion | flops 2620197888 | bytes 16199680 | tf_op jit(solution)/shard_map/cld,fd->clf/dot_general | solution.py:92
  255.2 3.0 fusion.133
  258.6 2.9 fusion.115
  263.1 2.5 convert_reduce_fusion.6
  265.7 7.8 convert_reduce_fusion.1
  273.5 3.7 multiply_reduce_fusion.5
  281.2 2.4 copy.55
  283.6 7.4 convolution_convert_fusion.1
  291.0 12.8 %multiply_reduce_fusion.1 = (f32[12,532]{1,0:T(8,128)S(1)}, f32[12,532,532]{1,2,0:T(8,128)}) fusion(f32[12,532,532]{1,2,0:T(8,128)} %get-tuple-element.80, f32[12,532]{1,0:T(8,128)S(1)} %copy-done.65, pred[532]{0:T(1024)(128)(4,1)S(1)} %get-tuple-element.33, bf16[532,12,64]{0,2,1:T(8,128)(2,1)S(1)} %bitcast.179, f32[532,12,64]{0,2,1:T(8,128)S(1)} %bitcast.159, ...), kind=kOutput, calls=%fused_computation.4 | convolution fusion | flops 452517056 | bytes 29676436 | tf_op jit(solution)/shard_map/clhe,cmhe->chlm/dot_general | solution.py:166
  303.8 12.5 %multiply_convert_fusion.1 = bf16[12,532,532]{1,2,0:T(8,128)(2,1)S(1)} fusion(f32[12,532,532]{1,2,0:T(8,128)} %get-tuple-element.89, f32[12,532,532]{1,2,0:T(8,128)} %get-tuple-element.80, f32[12,532]{1,0:T(8,128)S(1)} %get-tuple-element.88, f32[12,532]{1,0:T(8,128)S(1)} %copy-done.65, pred[532]{0:T(1024)(128)(4,1)S(1)} %get-tuple-element.33), kind=kLoop, calls=%fused_computation.3 | loop fusion | flops 20377728 | bytes 34014484 | tf_op jit(solution)/shard_map/convert_element_type | solution.py:170
  316.3 3.6 multiply_convert_fusion.4
  323.2 2.5 copy.60
  327.3 5.2 fusion.59
  336.2 8.0 convert_reduce_fusion
  344.3 6.8 multiply_reduce_fusion.3
  355.6 6.2 convolution_convert_fusion
  361.8 12.9 %multiply_reduce_fusion = (f32[12,532]{1,0:T(8,128)S(1)}, f32[12,532,532]{1,2,0:T(8,128)}) fusion(f32[12,532,532]{1,2,0:T(8,128)} %get-tuple-element.72, f32[12,532]{1,0:T(8,128)S(1)} %copy-done.63, pred[532]{0:T(1024)(128)(4,1)S(1)} %copy-done.83, bf16[532,12,64]{0,2,1:T(8,128)(2,1)S(1)} %bitcast.177, f32[532,12,64]{0,2,1:T(8,128)S(1)} %bitcast.157, ...), kind=kOutput, calls=%fused_computation.2 | convolution fusion | flops 452517056 | bytes 29676436 | tf_op jit(solution)/shard_map/clhe,cmhe->chlm/dot_general | solution.py:166
  374.7 12.5 %multiply_convert_fusion = bf16[12,532,532]{1,2,0:T(8,128)(2,1)S(1)} fusion(f32[12,532,532]{1,2,0:T(8,128)} %get-tuple-element.92, f32[12,532,532]{1,2,0:T(8,128)} %get-tuple-element.72, f32[12,532]{1,0:T(8,128)S(1)} %get-tuple-element.91, f32[12,532]{1,0:T(8,128)S(1)} %copy-done.63, pred[532]{0:T(1024)(128)(4,1)S(1)} %copy-done.83), kind=kLoop, calls=%fused_computation.1 | loop fusion | flops 20377728 | bytes 34014484 | tf_op jit(solution)/shard_map/convert_element_type | solution.py:170
  387.2 3.7 multiply_convert_fusion.2
  393.3 6.4 fusion.108
  399.8 7.2 fusion.119
  407.1 2.5 fusion.105
  409.7 5.1 fusion.75
  414.8 6.4 fusion.102
  421.2 7.0 fusion.122
  428.2 2.5 fusion.99
  435.3 5.5 fusion.58
  441.0 5.4 fusion.74
  451.3 33.5 %maximum_add_fusion = f32[9216,768]{1,0:T(8,128)} fusion(f32[3072,768]{1,0:T(8,128)} %fusion.108, f32[3072,768]{1,0:T(8,128)} %fusion.119, f32[768,768]{1,0:T(8,128)} %fusion.105, f32[2304,768]{1,0:T(8,128)} %bitcast.188, f32[3072,768]{1,0:T(8,128)} %fusion.102, f32[3072,768]{1,0:T(8,128)} %fusion.122, f32[768,768]{1,0:T(8,128)} %fusion.99, ...), kind=kLoop, calls=%fused_computation | loop fusion | flops 49545216 | bytes 84934656 | tf_op jit(solution)/shard_map/add | solution.py:276
  492.1 78.6 %all-reduce.3.cloned.1.call-done = (f32[10,768]{1,0:T(8,128)}, f32[12,768]{1,0:T(8,128)}) async-done(((f32[10,768]{1,0:T(8,128)}, f32[12,768]{1,0:T(8,128)}), (f32[10,768]{1,0:T(8,128)}, f32[12,768]{1,0:T(8,128)})) %all-reduce.3.cloned.1.call-update) | async-done | bytes 67600 | tf_op jit(solution)/shard_map/psum | solution.py:281
  573.6 268.1 %reduce-scatter.2.cloned.1.call-done = f32[288,768]{1,0:T(8,128)} async-done(((f32[9216,768]{1,0:T(8,128)}), f32[288,768]{1,0:T(8,128)}) %reduce-scatter.2.cloned.1.call-update) | async-done | bytes 884752 | tf_op jit(solution)/shard_map/reduce_scatter | solution.py:280
  841.7 3.4 multiply_add_fusion.2
  (365 shorter events, 66.0 us)
Async XLA Ops:
  7.2 110.4 %all-gather.2.cloned.1.call-start = ((), (), s32[]{:S(2)}) async-start(), calls=%async_computation.1 | async-start | bytes 14598144 | tf_op jit(solution)/shard_map/all_gather | solution.py:236
  9.2 561.4 %all-reduce.3.cloned.1.call-start = ((), (), s32[]{:S(2)}) async-start(), calls=%async_computation.3 | async-start | bytes 196608 | tf_op jit(solution)/shard_map/psum | solution.py:281
  10.0 226.8 %copy-start.104 = (f32[3072]{0:T(1024)}, f32[3072]{0:T(1024)S(1)}, u32[]{:S(2)}) copy-start(f32[3072]{0:T(1024)S(1)} %add.334) | copy-start | bytes 36868
  11.8 176.2 %copy-start.91 = (f32[768]{0:T(1024)}, f32[768]{0:T(1024)S(1)}, u32[]{:S(2)}) copy-start(f32[768]{0:T(1024)S(1)} %get-tuple-element.32) | copy-start | bytes 9220
  11.8 243.3 %copy-start.84 = (f32[768]{0:T(1024)}, f32[768]{0:T(1024)S(1)}, u32[]{:S(2)}) copy-start(f32[768]{0:T(1024)S(1)} %get-tuple-element.28) | copy-start | bytes 9220
  11.8 243.3 %copy-start.108 = (f32[768]{0:T(1024)}, f32[768]{0:T(1024)S(1)}, u32[]{:S(2)}) copy-start(f32[768]{0:T(1024)S(1)} %get-tuple-element.27) | copy-start | bytes 9220
  11.9 186.4 %copy-start.68 = (f32[12,64]{1,0:T(8,128)}, f32[12,64]{1,0:T(8,128)S(1)}, u32[]{:S(2)}) copy-start(f32[12,64]{1,0:T(8,128)S(1)} %add.322) | copy-start | bytes 9220
  12.1 132.4 %copy-start.82 = (pred[532]{0:T(1024)(128)(4,1)}, pred[532]{0:T(1024)(128)(4,1)S(1)}, u32[]{:S(2)}) copy-start(pred[532]{0:T(1024)(128)(4,1)S(1)} %get-tuple-element.34) | copy-start | bytes 1600
  15.4 104.4 %copy-start.45 = (f32[512,768]{1,0:T(8,128)}, f32[512,768]{1,0:T(8,128)S(1)}, u32[]{:S(2)}) copy-start(f32[512,768]{1,0:T(8,128)S(1)} %get-tuple-element.65) | copy-start | bytes 4718596
  15.4 104.4 %copy-start.78 = (f32[10,768]{1,0:T(8,128)S(1)}, f32[10,768]{1,0:T(8,128)}, u32[]{:S(2)}) copy-start(f32[10,768]{1,0:T(8,128)} %param.11) | copy-start | bytes 92164
  125.2 10.1 %copy-start.8 = (bf16[1,1,532,768]{2,3,1,0:T(8,128)(2,1)}, bf16[1,1,532,768]{2,3,1,0:T(8,128)(2,1)S(1)}, u32[]{:S(2)}) copy-start(bf16[1,1,532,768]{2,3,1,0:T(8,128)(2,1)S(1)} %copy.49) | copy-start | bytes 2451460
  127.4 7.9 copy-start.4
  144.5 10.1 %copy-start.62 = (f32[12,532]{1,0:T(8,128)}, f32[12,532]{1,0:T(8,128)S(1)}, u32[]{:S(2)}) copy-start(f32[12,532]{1,0:T(8,128)S(1)} %log_add_fusion.1) | copy-start | bytes 76612
  156.4 9.7 %slice-start = ((s8[14155776]{0:T(1024)(128)(4,1)}), s8[4194304]{0:T(1024)(128)(4,1)S(1)}, s32[]{:S(2)}) async-start(s8[14155776]{0:T(1024)(128)(4,1)} %bitcast.194), calls=%async_computation.4 | async-start | bytes 8388608
  156.4 9.7 %slice-start.1 = ((s8[14155776]{0:T(1024)(128)(4,1)}), s8[4194304]{0:T(1024)(128)(4,1)S(1)}, s32[]{:S(2)}) async-start(s8[14155776]{0:T(1024)(128)(4,1)} %bitcast.194), calls=%async_computation.5 | async-start | bytes 8388608
  156.4 9.7 %slice-start.2 = ((s8[14155776]{0:T(1024)(128)(4,1)}), s8[4194304]{0:T(1024)(128)(4,1)S(1)}, s32[]{:S(2)}) async-start(s8[14155776]{0:T(1024)(128)(4,1)} %bitcast.194), calls=%async_computation.6 | async-start | bytes 8388608
  165.8 18.9 %copy-start.19 = (f32[532,768]{1,0:T(8,128)}, f32[532,768]{1,0:T(8,128)S(1)}, u32[]{:S(2)}) copy-start(f32[532,768]{1,0:T(8,128)S(1)} %get-tuple-element.74) | copy-start | bytes 4902916
  165.8 18.9 %copy-start.87 = (f32[532]{0:T(1024)}, f32[532]{0:T(1024)S(1)}, u32[]{:S(2)}) copy-start(f32[532]{0:T(1024)S(1)} %broadcast_multiply_fusion.14) | copy-start | bytes 6388
  166.1 18.5 %copy-start.98 = (f32[532]{0:T(1024)}, f32[532]{0:T(1024)S(1)}, u32[]{:S(2)}) copy-start(f32[532]{0:T(1024)S(1)} %add_rsqrt_fusion.3) | copy-start | bytes 6388
  189.6 43.4 %copy-start.80 = (f32[10,768]{1,0:T(8,128)}, f32[10,768]{1,0:T(8,128)S(1)}, u32[]{:S(2)}) copy-start(f32[10,768]{1,0:T(8,128)S(1)} %fusion.92) | copy-start | bytes 92164
  196.1 10.1 %copy-start.10 = (bf16[1,1,532,768]{2,3,1,0:T(8,128)(2,1)}, bf16[1,1,532,768]{2,3,1,0:T(8,128)(2,1)S(1)}, u32[]{:S(2)}) copy-start(bf16[1,1,532,768]{2,3,1,0:T(8,128)(2,1)S(1)} %copy.53) | copy-start | bytes 2451460
  198.3 7.9 copy-start.6
  215.4 10.4 %copy-start.64 = (f32[12,532]{1,0:T(8,128)}, f32[12,532]{1,0:T(8,128)S(1)}, u32[]{:S(2)}) copy-start(f32[12,532]{1,0:T(8,128)S(1)} %log_add_fusion) | copy-start | bytes 76612
  227.7 9.1 %slice-start.4 = ((s8[14155776]{0:T(1024)(128)(4,1)}), s8[4194304]{0:T(1024)(128)(4,1)S(1)}, s32[]{:S(2)}) async-start(s8[14155776]{0:T(1024)(128)(4,1)} %bitcast.196), calls=%async_computation.8 | async-start | bytes 8388608
  227.7 9.1 %slice-start.5 = ((s8[14155776]{0:T(1024)(128)(4,1)}), s8[4194304]{0:T(1024)(128)(4,1)S(1)}, s32[]{:S(2)}) async-start(s8[14155776]{0:T(1024)(128)(4,1)} %bitcast.196), calls=%async_computation.9 | async-start | bytes 8388608
  227.7 9.1 %slice-start.6 = ((s8[14155776]{0:T(1024)(128)(4,1)}), s8[4194304]{0:T(1024)(128)(4,1)S(1)}, s32[]{:S(2)}) async-start(s8[14155776]{0:T(1024)(128)(4,1)} %bitcast.196), calls=%async_computation.10 | async-start | bytes 8388608
  236.4 40.7 %copy-start.22 = (f32[532,768]{1,0:T(8,128)}, f32[532,768]{1,0:T(8,128)S(1)}, u32[]{:S(2)}) copy-start(f32[532,768]{1,0:T(8,128)S(1)} %get-tuple-element.82) | copy-start | bytes 4902916
  236.4 40.7 %copy-start.89 = (f32[532]{0:T(1024)}, f32[532]{0:T(1024)S(1)}, u32[]{:S(2)}) copy-start(f32[532]{0:T(1024)S(1)} %broadcast_multiply_fusion.12) | copy-start | bytes 6388
  236.8 40.3 %copy-start.100 = (f32[532]{0:T(1024)}, f32[532]{0:T(1024)S(1)}, u32[]{:S(2)}) copy-start(f32[532]{0:T(1024)S(1)} %add_rsqrt_fusion.1) | copy-start | bytes 6388
  265.6 7.8 copy-start.40
  265.7 7.8 copy-start.85
  303.8 12.5 %copy-start.7 = (f32[1,1,532,768]{2,3,1,0:T(8,128)S(1)}, f32[1,1,532,768]{2,3,1,0:T(8,128)}, u32[]{:S(2)}) copy-start(f32[1,1,532,768]{2,3,1,0:T(8,128)} %copy-done.6) | copy-start | bytes 4902916
  303.8 12.5 %copy-start.69 = (f32[12,64]{1,0:T(8,128)S(1)}, f32[12,64]{1,0:T(8,128)}, u32[]{:S(2)}) copy-start(f32[12,64]{1,0:T(8,128)} %copy-done.68) | copy-start | bytes 9220
  323.2 9.4 %copy-start.55 = (bf16[1,532,768]{2,1,0:T(8,128)(2,1)}, bf16[1,532,768]{2,1,0:T(8,128)(2,1)S(1)}, u32[]{:S(2)}) copy-start(bf16[1,532,768]{2,1,0:T(8,128)(2,1)S(1)} %copy.61) | copy-start | bytes 2451460
  336.1 8.1 copy-start.42
  336.1 8.1 copy-start.20
  336.1 8.1 copy-start.86
  336.1 8.1 copy-start.88
  336.1 8.1 copy-start.99
  374.7 12.5 %copy-start.5 = (f32[1,1,532,768]{2,3,1,0:T(8,128)S(1)}, f32[1,1,532,768]{2,3,1,0:T(8,128)}, u32[]{:S(2)}) copy-start(f32[1,1,532,768]{2,3,1,0:T(8,128)} %copy-done.4) | copy-start | bytes 4902916
  374.7 12.5 %copy-start.70 = (f32[12,64]{1,0:T(8,128)S(1)}, f32[12,64]{1,0:T(8,128)}, u32[]{:S(2)}) copy-start(f32[12,64]{1,0:T(8,128)} %copy-done.68) | copy-start | bytes 9220
  451.3 390.4 %reduce-scatter.2.cloned.1.call-start = ((), (), s32[]{:S(2)}) async-start(), calls=%async_computation.2 | async-start | bytes 29196288 | tf_op jit(solution)/shard_map/reduce_scatter | solution.py:280
  490.2 81.9 %copy-start.71 = (f32[12,768]{1,0:T(8,128)S(1)}, f32[12,768]{1,0:T(8,128)}, u32[]{:S(2)}) copy-start(f32[12,768]{1,0:T(8,128)} %param.17) | copy-start | bytes 110596
  490.2 81.9 %copy-start.76 = (f32[12,768]{1,0:T(8,128)S(1)}, f32[12,768]{1,0:T(8,128)}, u32[]{:S(2)}) copy-start(f32[12,768]{1,0:T(8,128)} %param.18) | copy-start | bytes 110596
  490.2 81.9 %copy-start.77 = (f32[12,768]{1,0:T(8,128)S(1)}, f32[12,768]{1,0:T(8,128)}, u32[]{:S(2)}) copy-start(f32[12,768]{1,0:T(8,128)} %param.19) | copy-start | bytes 110596
  490.2 351.5 %copy-start.35 = (f32[288,768]{1,0:T(8,128)S(1)}, f32[288,768]{1,0:T(8,128)}, u32[]{:S(2)}) copy-start(f32[288,768]{1,0:T(8,128)} %param.14) | copy-start | bytes 2654212
  490.2 351.5 %copy-start.53 = (f32[288,768]{1,0:T(8,128)S(1)}, f32[288,768]{1,0:T(8,128)}, u32[]{:S(2)}) copy-start(f32[288,768]{1,0:T(8,128)} %param.15) | copy-start | bytes 2654212
  490.2 351.5 %copy-start.54 = (f32[288,768]{1,0:T(8,128)S(1)}, f32[288,768]{1,0:T(8,128)}, u32[]{:S(2)}) copy-start(f32[288,768]{1,0:T(8,128)} %param.16) | copy-start | bytes 2654212
  (86 other events, 397.7 us)
Sparse Core Ops, SparseCore 0:
  11.6 105.9 all-gather.1
  451.4 119.1 all-reduce.2
  577.1 264.5 reduce-scatter.1
where the time goes:
time: 856 us; the launch traced here: 852 us
  waiting for transfers between devices  449 us (52%)
  matrix products  214 us (25%)
  other arithmetic  131 us (15%)
  local copies, waits for them, and re-layouts  41.6 us (5%)
  between operations  16.6 us (2%)
    reduce_scatter x1, waiting for transfers between devices, shards(): lax.psum_scatter(matrix_total, ('dp', 'fsdp'), scatter_dimension=0, tiled...  268 us
    all_gather x1, waiting for transfers between devices, shards(): lax.all_gather(weight_shard, ('dp', 'fsdp'), axis=0, tiled=True)  102 us
    psum x1, waiting for transfers between devices, shards(): lax.psum((vector_total, memory_local), ('dp', 'fsdp'))  78.6 us
    dot_general x2, matrix products, forward_segment(): jnp.einsum('cld,fd->clf', first_low, w_up, preferred_element_type=jnp.flo...  36.6 us
    add x1, other arithmetic, shards(): matrix_total = matrix_total + matrix_grad  33.5 us
    dot_general x2, matrix products, backward_segment(): jnp.einsum('clhe,cmhe->chlm', attended_grad, value_rows, preferred_elemen...  25.7 us
    convert_element_type x2, other arithmetic, backward_segment(): score_low = (soft_full * (soft_grad - row_inner)).astype(jnp.bfloat16)  24.9 us
    convert_element_type x2, other arithmetic, forward_segment(): soft_low = jnp.exp(scores - log_total).astype(jnp.bfloat16)  20.5 us
  transfers between devices with their start and end apart: 3, of which 3 were waited for; matrix products, arithmetic and copies ran while one was open for 5% of the time, Pallas kernels for 0%

commit v1 on v0

v1 whole, which is shorter than its diff:
```python
import functools

import jax
import jax.numpy as jnp
from jax import lax
from jax.experimental import pallas as pl
from jax.experimental.pallas import tpu as pltpu
from jax.sharding import PartitionSpec as P

D = 768
HEADS = 12
HEAD = 64
FF = 3072
MEM = 10
SEG_LEN = 512
SEGS = 2
PADM = 16
ROWS = SEG_LEN + 2 * PADM
ROWS_LANES = -(-ROWS // 128) * 128
COLS = 256
STEPS = D // COLS
CHUNKS = FF // D

eps_norm = 1e-12
beta_one = 0.9
beta_two = 0.95
decay_rate = 0.1
adam_eps = 1e-08
adam_step = 10
neg_large = -1e30
LOG2E = 1.4426950408889634
SCORE2 = HEAD ** (-0.5) * LOG2E
ROOT = HEAD ** (-0.5)
f32 = jnp.float32
bf16 = jnp.bfloat16
VMEM_BYTES = 56 * 1024 * 1024


def dot_nn(left, right):
    return lax.dot_general(left, right, (((1,), (0,)), ((), ())), preferred_element_type=f32)


def dot_nt(left, right):
    return lax.dot_general(left, right, (((1,), (1,)), ((), ())), preferred_element_type=f32)


def dot_tn(left, right):
    return lax.dot_general(left, right, (((0,), (0,)), ((), ())), preferred_element_type=f32)


def valid_positions(shape, axis, live):
    at = lax.broadcasted_iota(jnp.int32, shape, axis)
    read = (at >= SEG_LEN) & (at < SEG_LEN + MEM)
    write = (at >= SEG_LEN + PADM) & (at < SEG_LEN + PADM + MEM)
    return (at < live) | read | write


def mask_half(values, half):
    lane = lax.broadcasted_iota(jnp.int32, values.shape, 1)
    keep = (lane < HEAD) if half == 0 else (lane >= HEAD)
    return jnp.where(keep, values, jnp.zeros_like(values))


def norm_rows(values):
    centred = values - jnp.mean(values, axis=-1, keepdims=True)
    inverse = lax.rsqrt(jnp.mean(centred * centred, axis=-1, keepdims=True) + eps_norm)
    return centred * inverse, inverse


def norm_back(gradient, normed, inverse, gain_row):
    scaled = gradient * gain_row
    centred = scaled - jnp.mean(scaled, axis=-1, keepdims=True)
    return inverse * (centred - normed * jnp.mean(scaled * normed, axis=-1, keepdims=True))


def gelu_parts(z):
    gauss = jnp.exp2(z * z * (-0.5 * LOG2E))
    base = 1.0 + jnp.abs(z) * (0.3275911 * 0.7071067811865476)
    t = pl.reciprocal(base, approx=True)
    t = t * (2.0 - base * t)
    poly = 0.5 * 1.061405429
    poly = poly * t + 0.5 * -1.453152027
    poly = poly * t + 0.5 * 1.421413741
    poly = poly * t + 0.5 * -0.284496736
    poly = poly * t + 0.5 * 0.254829592
    tail = poly * t * gauss
    phi = jnp.where(z >= 0.0, 1.0 - tail, tail)
    return z * phi, phi + z * gauss * 0.3989422804014327


def attn_fwd_kernel(
    live_ref, tok_ref, mem_ref, wq_ref, wk_ref, wv_ref, vec_ref,
    x_ref, q_ref, k_ref, v_ref, lse_ref, a_ref, lse_acc,
):
    step = pl.program_id(0)
    live = live_ref[0]

    @pl.when(step == 0)
    def _():
        x_ref[0:SEG_LEN] = tok_ref[...]
        low = mem_ref[...].astype(bf16)
        x_ref[SEG_LEN:SEG_LEN + PADM] = low
        x_ref[SEG_LEN + PADM:ROWS] = low
        lse_acc[...] = jnp.zeros_like(lse_acc)

    x = x_ref[...]
    q = (dot_nn(x, wq_ref[...]) + vec_ref[0:1]).astype(bf16)
    k = dot_nn(x, wk_ref[...]).astype(bf16)
    v = (dot_nn(x, wv_ref[...]) + vec_ref[1:2]).astype(bf16)
    q_ref[...] = q
    k_ref[...] = k
    v_ref[...] = v
    valid = valid_positions((1, ROWS), 1, live)
    lane = lax.broadcasted_iota(jnp.int32, (1, 128), 1)
    lse_all = lse_acc[0:ROWS]
    for pair in range(COLS // 128):
        cols = slice(128 * pair, 128 * pair + 128)
        qp, kp, vp = q[:, cols], k[:, cols], v[:, cols]
        total = None
        for half in range(2):
            s = dot_nt(qp, mask_half(kp, half))
            s = jnp.where(valid, s, neg_large)
            top = jnp.max(s, axis=1, keepdims=True)
            e = jnp.exp2((s - top) * SCORE2)
            amount = jnp.sum(e, axis=1, keepdims=True)
            p = (e * (1.0 / amount)).astype(bf16)
            lse = top * SCORE2 + jnp.log(amount) * LOG2E
            head = step * (COLS // HEAD) + 2 * pair + half
            lse_all = jnp.where(lane == head, lse, lse_all)
            part = dot_nn(p, mask_half(vp, half))
            total = part if total is None else total + part
        a_ref[:, cols] = total.astype(bf16)
    lse_acc[0:ROWS] = lse_all

    @pl.when(step == STEPS - 1)
    def _():
        lse_ref[...] = lse_acc[...].T[0:16]


def ffn_fwd_kernel(
    live_ref, tok_ref, mem_ref, a_ref, wo_ref, wu_ref, wd_ref, vec_ref,
    n1_ref, i1_ref, h1b_ref, g_ref, slope_ref, n2_ref, i2_ref, out_ref, next_ref,
    h1, acc,
):
    step = pl.program_id(0)
    live = live_ref[0]

    @pl.when(step == 0)
    def _():
        branch = dot_nn(a_ref[...], wo_ref[...]) + vec_ref[2:3]
        mem = mem_ref[...]
        u = jnp.concatenate([tok_ref[...].astype(f32), mem, mem], axis=0)
        normed, inverse = norm_rows(u + branch)
        n1_ref[...] = normed
        i1_ref[...] = inverse
        full = normed * vec_ref[3:4] + vec_ref[4:5]
        h1[...] = full
        h1b_ref[...] = full.astype(bf16)
        acc[...] = full + vec_ref[5:6]

    z = dot_nt(h1b_ref[...], wu_ref[...]) + vec_ref[pl.ds(8 + step, 1), :]
    g, slope = gelu_parts(z)
    g = g.astype(bf16)
    g_ref[...] = g
    slope_ref[...] = slope
    acc[...] += dot_nn(g, wd_ref[...])

    @pl.when(step == CHUNKS - 1)
    def _():
        normed, inverse = norm_rows(acc[...])
        n2_ref[...] = normed
        i2_ref[...] = inverse
        y = normed * vec_ref[6:7] + vec_ref[7:8]
        row = lax.broadcasted_iota(jnp.int32, (SEG_LEN, 1), 0)
        out_ref[...] = jnp.where(row < live, y[0:SEG_LEN], 0.0)
        next_ref[...] = jnp.where(live > 0, y[SEG_LEN + PADM:ROWS], mem_ref[...])


def ffn_bwd_kernel(
    live_ref, cot_ref, dmem_ref, n1_ref, i1_ref, n2_ref, i2_ref, slope_ref, wo_ref, wu_ref, wd_ref, vec_ref,
    dfb_ref, dzb_ref, dob_ref, dr1_ref, da_ref, sums_ref,
    acc,
):
    step = pl.program_id(0)
    live = live_ref[0]

    @pl.when(step == 0)
    def _():
        row = lax.broadcasted_iota(jnp.int32, (SEG_LEN, 1), 0)
        token = jnp.where(row < live, cot_ref[...].astype(f32), 0.0)
        write = jnp.where(live > 0, dmem_ref[...], 0.0)
        dy = jnp.concatenate([token, jnp.zeros((PADM, D), f32), write], axis=0)
        normed = n2_ref[...]
        sums_ref[...] = jnp.zeros_like(sums_ref)
        sums_ref[6:7] = jnp.sum(dy * normed, axis=0, keepdims=True)
        sums_ref[7:8] = jnp.sum(dy, axis=0, keepdims=True)
        back = norm_back(dy, normed, i2_ref[...], vec_ref[6:7])
        low = back.astype(bf16)
        dfb_ref[...] = low
        sums_ref[5:6] = jnp.sum(low.astype(f32), axis=0, keepdims=True)
        acc[...] = back

    dz = (dot_nt(dfb_ref[...], wd_ref[...]) * slope_ref[...]).astype(bf16)
    dzb_ref[...] = dz
    sums_ref[pl.ds(8 + step, 1), :] = jnp.sum(dz.astype(f32), axis=0, keepdims=True)
    acc[...] += dot_nn(dz, wu_ref[...])

    @pl.when(step == CHUNKS - 1)
    def _():
        dh = acc[...]
        normed = n1_ref[...]
        sums_ref[3:4] = jnp.sum(dh * normed, axis=0, keepdims=True)
        sums_ref[4:5] = jnp.sum(dh, axis=0, keepdims=True)
        back = norm_back(dh, normed, i1_ref[...], vec_ref[3:4])
        dr1_ref[...] = back
        low = back.astype(bf16)
        dob_ref[...] = low
        sums_ref[2:3] = jnp.sum(low.astype(f32), axis=0, keepdims=True)
        da_ref[...] = dot_nt(low, wo_ref[...]).astype(bf16)


def attn_bwd_kernel(
    live_ref, q_ref, k_ref, v_ref, da_ref, lse_ref, dr1_ref, wq_ref, wk_ref, wv_ref,
    dq_ref, dk_ref, dv_ref, sums_ref, du_ref,
):
    step = pl.program_id(0)
    live = live_ref[0]

    @pl.when(step == 0)
    def _():
        du_ref[...] = dr1_ref[...]

    valid = valid_positions((ROWS, 1), 0, live)
    for pair in range(COLS // 128):
        cols = slice(128 * pair, 128 * pair + 128)
        qp, kp, vp, dap = q_ref[:, cols], k_ref[:, cols], v_ref[:, cols], da_ref[:, cols]
        dq = dk = dv = None
        for half in range(2):
            head = step * (COLS // HEAD) + 2 * pair + half
            kh, vh, qh, dah = (mask_half(t, half) for t in (kp, vp, qp, dap))
            s = dot_nt(kh, qp)
            s = jnp.where(valid, s, neg_large)
            p = jnp.exp2(s * SCORE2 - lse_ref[pl.ds(head, 1), 0:ROWS])
            dp = dot_nt(vh, dap)
            inner = jnp.sum(p * dp, axis=0, keepdims=True)
            ds = (p * (dp - inner)).astype(bf16)
            parts = (dot_tn(ds, kh), dot_nn(ds, qh), dot_nn(p.astype(bf16), dah))
            if dq is None:
                dq, dk, dv = parts
            else:
                dq, dk, dv = dq + parts[0], dk + parts[1], dv + parts[2]
        dq_ref[:, cols] = (dq * ROOT).astype(bf16)
        dk_ref[:, cols] = (dk * ROOT).astype(bf16)
        dv_ref[:, cols] = dv.astype(bf16)
    dq, dk, dv = dq_ref[...], dk_ref[...], dv_ref[...]
    sums_ref[0:1] = jnp.sum(dq.astype(f32), axis=0, keepdims=True)
    sums_ref[1:2] = jnp.sum(dv.astype(f32), axis=0, keepdims=True)
    du_ref[...] += dot_nt(dq, wq_ref[...]) + dot_nt(dk, wk_ref[...]) + dot_nt(dv, wv_ref[...])


def grad_ffn_kernel(dz0_ref, dz1_ref, g0_ref, g1_ref, h0_ref, h1_ref, df0_ref, df1_ref, out_ref):
    step = pl.program_id(0)

    @pl.when(step < CHUNKS)
    def _():
        out_ref[...] = (dot_tn(dz0_ref[...], h0_ref[...]) + dot_tn(dz1_ref[...], h1_ref[...])).astype(bf16)

    @pl.when(step >= CHUNKS)
    def _():
        out_ref[...] = (dot_tn(g0_ref[...], df0_ref[...]) + dot_tn(g1_ref[...], df1_ref[...])).astype(bf16)


def grad_attn_kernel(x0_ref, x1_ref, a0_ref, a1_ref, r0_ref, r1_ref, k0_ref, k1_ref, v0_ref, v1_ref, o0_ref, o1_ref, out_ref):
    step = pl.program_id(0)
    for index, (left0, left1, right0, right1) in enumerate((
        (x0_ref, x1_ref, r0_ref, r1_ref), (x0_ref, x1_ref, k0_ref, k1_ref),
        (x0_ref, x1_ref, v0_ref, v1_ref), (a0_ref, a1_ref, o0_ref, o1_ref),
    )):
        @pl.when(step == index)
        def _(left0=left0, left1=left1, right0=right0, right1=right1):
            out_ref[...] = (dot_tn(left0[...], right0[...]) + dot_tn(left1[...], right1[...])).astype(bf16)


def spec(shape, index):
    return pl.BlockSpec(shape, index)


def whole(shape):
    return pl.BlockSpec(shape, lambda j: (0,) * len(shape))


SCALAR = pl.BlockSpec(memory_space=pltpu.SMEM)


def shape_of(shape, dtype):
    return jax.ShapeDtypeStruct(shape, dtype)


def params():
    return pltpu.CompilerParams(dimension_semantics=("arbitrary",), vmem_limit_bytes=VMEM_BYTES)


def cost(flops, moved):
    return pl.CostEstimate(flops=int(flops), bytes_accessed=int(moved), transcendentals=0)


def attn_fwd(segment, live, tokens, mem, weights, vectors):
    block = spec((ROWS, COLS), lambda j: (0, j))
    return pl.pallas_call(
        attn_fwd_kernel,
        grid=(STEPS,),
        in_specs=[
            SCALAR, spec((SEG_LEN, D), lambda j: (segment, 0)), whole((PADM, D)),
            spec((D, COLS), lambda j: (0, j)), spec((D, COLS), lambda j: (1, j)), spec((D, COLS), lambda j: (2, j)),
            spec((12, COLS), lambda j: (0, j)),
        ],
        out_specs=[whole((ROWS, D)), block, block, block, whole((16, ROWS_LANES)), block],
        out_shape=[shape_of((ROWS, D), bf16)] * 4 + [shape_of((16, ROWS_LANES), f32), shape_of((ROWS, D), bf16)],
        scratch_shapes=[pltpu.VMEM((ROWS_LANES, 128), f32)],
        compiler_params=params(),
        name="attn_fwd",
        cost_estimate=cost(5e9, 8e6),
    )(live, tokens, mem, weights, weights, weights, vectors)


def ffn_fwd(segment, live, tokens, mem, attended, weights, vectors):
    full = whole((ROWS, D))
    chunk = spec((ROWS, D), lambda j: (0, j))
    col = whole((ROWS, 1))
    return pl.pallas_call(
        ffn_fwd_kernel,
        grid=(CHUNKS,),
        in_specs=[
            SCALAR, spec((SEG_LEN, D), lambda j: (segment, 0)), whole((PADM, D)), full,
            spec((D, D), lambda j: (3, 0)), spec((D, D), lambda j: (4 + j, 0)), spec((D, D), lambda j: (8 + j, 0)),
            whole((12, D)),
        ],
        out_specs=[full, col, full, chunk, chunk, full, col, whole((SEG_LEN, D)), whole((PADM, D))],
        out_shape=[
            shape_of((ROWS, D), f32), shape_of((ROWS, 1), f32), shape_of((ROWS, D), bf16), shape_of((ROWS, FF), bf16),
            shape_of((ROWS, FF), f32), shape_of((ROWS, D), f32), shape_of((ROWS, 1), f32),
            shape_of((SEG_LEN, D), f32), shape_of((PADM, D), f32),
        ],
        scratch_shapes=[pltpu.VMEM((ROWS, D), f32)] * 2,
        compiler_params=params(),
        name="ffn_fwd",
        cost_estimate=cost(6e9, 25e6),
    )(live, tokens, mem, attended, weights, weights, weights, vectors)


def ffn_bwd(segment, live, cotangent, dmem, saved, weights, vectors):
    n1, i1, h1b, g, slope, n2, i2 = saved
    full = whole((ROWS, D))
    chunk = spec((ROWS, D), lambda j: (0, j))
    col = whole((ROWS, 1))
    return pl.pallas_call(
        ffn_bwd_kernel,
        grid=(CHUNKS,),
        in_specs=[
            SCALAR, spec((SEG_LEN, D), lambda j: (segment, 0)), whole((PADM, D)), full, col, full, col, chunk,
            spec((D, D), lambda j: (3, 0)), spec((D, D), lambda j: (4 + j, 0)), spec((D, D), lambda j: (8 + j, 0)),
            whole((12, D)),
        ],
        out_specs=[full, chunk, full, full, full, whole((12, D))],
        out_shape=[
            shape_of((ROWS, D), bf16), shape_of((ROWS, FF), bf16), shape_of((ROWS, D), bf16),
            shape_of((ROWS, D), f32), shape_of((ROWS, D), bf16), shape_of((12, D), f32),
        ],
        scratch_shapes=[pltpu.VMEM((ROWS, D), f32)],
        compiler_params=params(),
        name="ffn_bwd",
        cost_estimate=cost(6e9, 25e6),
    )(live, cotangent, dmem, n1, i1, n2, i2, slope, weights, weights, weights, vectors)


def attn_bwd(live, q, k, v, da, lse, dr1, weights):
    block = spec((ROWS, COLS), lambda j: (0, j))
    return pl.pallas_call(
        attn_bwd_kernel,
        grid=(STEPS,),
        in_specs=[
            SCALAR, block, block, block, block, whole((16, ROWS_LANES)), whole((ROWS, D)),
            spec((D, COLS), lambda j: (0, j)), spec((D, COLS), lambda j: (1, j)), spec((D, COLS), lambda j: (2, j)),
        ],
        out_specs=[block, block, block, spec((8, COLS), lambda j: (0, j)), whole((ROWS, D))],
        out_shape=[shape_of((ROWS, D), bf16)] * 3 + [
            shape_of((8, D), f32), shape_of((ROWS, D), f32)],
        compiler_params=params(),
        name="attn_bwd",
        cost_estimate=cost(10e9, 10e6),
    )(live, q, k, v, da, lse, dr1, weights, weights, weights)


def grad_ffn(dz, g, h, df):
    up = spec((ROWS, D), lambda j: (0, jnp.minimum(j, CHUNKS - 1)))
    down = spec((ROWS, D), lambda j: (0, jnp.maximum(j - CHUNKS, 0)))
    full = whole((ROWS, D))
    return pl.pallas_call(
        grad_ffn_kernel,
        grid=(2 * CHUNKS,),
        in_specs=[up, up, down, down, full, full, full, full],
        out_specs=spec((D, D), lambda j: (j, 0)),
        out_shape=shape_of((2 * FF, D), bf16),
        compiler_params=params(),
        name="grad_ffn",
        cost_estimate=cost(10e9, 25e6),
    )(*dz, *g, *h, *df)


def grad_attn(x, a, dq, dk, dv, do):
    full = whole((ROWS, D))
    return pl.pallas_call(
        grad_attn_kernel,
        grid=(4,),
        in_specs=[full] * 12,
        out_specs=spec((D, D), lambda j: (j, 0)),
        out_shape=shape_of((4 * D, D), bf16),
        compiler_params=params(),
        name="grad_attn",
        cost_estimate=cost(5e9, 15e6),
    )(*x, *a, *dq, *dk, *dv, *do)


def adam_update(parameter, gradient, moment_one, moment_two, decay_factor):
    new_one = beta_one * moment_one + (1.0 - beta_one) * gradient
    new_two = beta_two * moment_two + (1.0 - beta_two) * gradient * gradient
    corrected_one = new_one / (1.0 - beta_one**adam_step)
    corrected_two = new_two / (1.0 - beta_two**adam_step)
    update = corrected_one / (jnp.sqrt(corrected_two) + adam_eps) + decay_factor * parameter
    return (update, new_one, new_two)


def local_grads(tokens, memory_init, chain_tokens, cotangent, weights, vectors):
    mem = jnp.pad(memory_init, ((0, PADM - MEM), (0, 0)))
    lives = [jnp.clip(chain_tokens - s * SEG_LEN, 0, SEG_LEN) for s in range(SEGS)]
    kept = []
    outputs = []
    for s in range(SEGS):
        x, q, k, v, lse, a = attn_fwd(s, lives[s], tokens, mem, weights, vectors)
        *saved, out, mem = ffn_fwd(s, lives[s], tokens, mem, a, weights, vectors)
        kept.append((x, q, k, v, lse, a, saved))
        outputs.append(out)
    dmem = jnp.zeros((PADM, D), f32)
    back = [None] * SEGS
    token_grads = [None] * SEGS
    for s in reversed(range(SEGS)):
        x, q, k, v, lse, a, saved = kept[s]
        dfb, dzb, dob, dr1, da, sums = ffn_bwd(s, lives[s], cotangent, dmem, saved, weights, vectors)
        dq, dk, dv, sums_qv, du = attn_bwd(lives[s], q, k, v, da, lse, dr1, weights)
        token_grads[s] = du[:SEG_LEN]
        dmem = du[SEG_LEN:SEG_LEN + PADM] + du[SEG_LEN + PADM:] + jnp.where(lives[s] > 0, 0.0, dmem)
        back[s] = (dfb, dzb, dob, dq, dk, dv, sums, sums_qv)
    pick = lambda items, i: [item[i] for item in items]
    wide = grad_ffn(pick(back, 1), [k_[6][3] for k_ in kept], [k_[6][2] for k_ in kept], pick(back, 0))
    square = grad_attn(pick(kept, 0), pick(kept, 5), pick(back, 3), pick(back, 4), pick(back, 5), pick(back, 2))
    sums = sum(pick(back, 6))
    sums_qv = sum(pick(back, 7))
    vector_total = jnp.concatenate([sums_qv[0:2], sums[2:]], axis=0)
    return (jnp.concatenate(outputs, 0), jnp.concatenate(token_grads, 0), dmem[:MEM], square, wide, vector_total)


def shards(
    tokens, memory_init, chain_tokens, cotangent, weights, weight_first, weight_second,
    vectors, vector_first, vector_second,
):
    axes = ("dp", "fsdp")
    total_chains = tokens.shape[0] * lax.axis_size(axes)
    grad_scale = float(total_chains * SEGS * SEG_LEN) ** (-0.5)
    gathered = lax.all_gather(weights.astype(bf16), axes, axis=0, tiled=True)
    output, token_grad, memory_local, square, wide, vector_total = local_grads(
        tokens[0], memory_init, chain_tokens, cotangent[0], gathered, vectors)
    matrix_total = jnp.concatenate([square, wide], axis=0)
    weight_sum = lax.psum_scatter(matrix_total, axes, scatter_dimension=0, tiled=True).astype(f32)
    vector_sum, memory_sum = lax.psum((vector_total, memory_local), axes)
    weight_grad = weight_sum * grad_scale
    vector_grad = vector_sum * grad_scale
    memory_grad = memory_sum * grad_scale
    weight_step, new_weight_first, new_weight_second = adam_update(
        weights, weight_grad, weight_first, weight_second, decay_rate)
    vector_step, new_vector_first, new_vector_second = adam_update(
        vectors, vector_grad, vector_first, vector_second, 0.0)
    return (
        output[None], token_grad[None], memory_grad, weight_grad, weight_step, new_weight_first, new_weight_second,
        vector_grad, vector_step, new_vector_first, new_vector_second,
    )


def solution(mesh):
    both = ("dp", "fsdp")
    chain = P(both, None, None)
    rows = P(both, None)
    return jax.shard_map(
        shards,
        mesh=mesh,
        in_specs=(chain, P(), P(both), chain, rows, rows, rows, P(), P(), P()),
        out_specs=(chain, chain, P(), rows, rows, rows, rows, P(), P(), P(), P()),
        check_vma=False,
    )
```

time: 856 us -> 574 us (0.67)
  matrix products: 214 us -> 0 us
  Pallas kernels: 0 us -> 177 us
  waiting for transfers between devices: 449 us -> 334 us
  other arithmetic: 131 us -> 31.7 us
  local copies, waits for them, and re-layouts: 41.6 us -> 6.72 us
    dot_general x36 -> x0, matrix products: 214 us -> none  [the longest x2 36.6 us: forward_segment(): jnp.einsum('cld,fd->clf', first_low, w_up, preferred_element_type=jnp.flo...]
    pallas_call x0 -> x10, Pallas kernels: none -> 177 us  [the longest x2 41.1 us: attn_bwd(): pl.pallas_call(attn_bwd_kernel, grid=(STEPS,), in_specs=[SCALAR, block, b...]
    reduce_scatter x1, waiting for transfers between devices: 268 us -> 167 us  [shards(): lax.psum_scatter(matrix_total, axes, scatter_dimension=0, tiled=True)]
    convert_element_type x5 -> x1, other arithmetic: 47.4 us -> 1.98 us  [shards(): gathered = lax.all_gather(weights.astype(bf16), axes, axis=0, tiled=True)]
    reduce_sum x20 -> x0, other arithmetic: 34.9 us -> none  [the longest x2 18.3 us: forward_segment(): jnp.sum(jnp.exp(scores - row_max), axis=-1, keepdims=True)]
    add x5 -> x4, other arithmetic: 34.5 us -> 2.85 us  [the longest x2 2.08 us: local_grads(): du[SEG_LEN:SEG_LEN + PADM] + du[SEG_LEN + PADM:]]
    psum x1, waiting for transfers between devices: 78.6 us -> 61.1 us  [shards(): vector_sum, memory_sum = lax.psum((vector_total, memory_local), axes)]
    slice x17 -> x3, local copies, waits for them, and re-layouts: 18.1 us -> 1.04 us  [the longest x1 0.83 us: local_grads(): du[SEG_LEN:SEG_LEN + PADM] + du[SEG_LEN + PADM:]]
  transfers between devices with their start and end apart: 3 -> 3, of which waited for: 3 -> 3; matrix products, arithmetic and copies ran while one was open for 5% -> 4% of each run, Pallas kernels for 0% -> 6%
where the time goes in v1:
time: 574 us; the launch traced here: 564 us
  waiting for transfers between devices  334 us (58%)
  Pallas kernels  177 us (31%)
  other arithmetic  31.7 us (6%)
  between operations  14.7 us (3%)
  local copies, waits for them, and re-layouts  6.72 us (1%)
    reduce_scatter x1, waiting for transfers between devices, shards(): lax.psum_scatter(matrix_total, axes, scatter_dimension=0, tiled=True)  167 us
    all_gather x1, waiting for transfers between devices, shards(): gathered = lax.all_gather(weights.astype(bf16), axes, axis=0, tiled=True)  106 us
    psum x1, waiting for transfers between devices, shards(): vector_sum, memory_sum = lax.psum((vector_total, memory_local), axes)  61.1 us
    pallas_call x2, Pallas kernels, attn_bwd(): pl.pallas_call(attn_bwd_kernel, grid=(STEPS,), in_specs=[SCALAR, block, b...  41.1 us
    pallas_call x2, Pallas kernels, ffn_fwd(): pl.pallas_call(ffn_fwd_kernel, grid=(CHUNKS,), in_specs=[SCALAR, spec((SE...  38.9 us
    pallas_call x2, Pallas kernels, ffn_bwd(): pl.pallas_call(ffn_bwd_kernel, grid=(CHUNKS,), in_specs=[SCALAR, spec((SE...  33.7 us
    pallas_call x2, Pallas kernels, attn_fwd(): pl.pallas_call(attn_fwd_kernel, grid=(STEPS,), in_specs=[SCALAR, spec((SE...  28.6 us
    pallas_call x1, Pallas kernels, grad_ffn(): pl.pallas_call(grad_ffn_kernel, grid=(2 * CHUNKS,), in_specs=[up, up, dow...  21.1 us
  transfers between devices with their start and end apart: 3, of which 3 were waited for; matrix products, arithmetic and copies ran while one was open for 4% of the time, Pallas kernels for 6%

profile of v1, /device:TPU:0, one launch (start us, length us, event | category | flops | bytes accessed | tf_op | source)
XLA Modules:
  0.0 564.2 jit_solution(14061044575973079267)
XLA Ops:
  7.2 0.0 all-gather.2.cloned.1.call-start
  7.2 2.0 convert_element_type.8
  9.2 0.0 all-gather.2.cloned.1.call-update
  9.2 0.0 all-reduce.4.cloned.1.call-start
  9.9 1.4 pad.4.mem_ref
  11.4 106.3 %all-gather.2.cloned.1.call-done.wq_ref.wk_ref.wv_ref.wo_ref.wu_ref.wd_ref = bf16[9216,768]{1,0:T(8,128)(2,1)} async-done(((bf16[288,768]{1,0:T(8,128)(2,1)}), bf16[9216,768]{1,0:T(8,128)(2,1)}) %all-gather.2.cloned.1.call-update) | async-done | bytes 14155792 | tf_op jit(solution)/shard_map/all_gather | solution.py:469
  117.6 14.3 %attn_fwd.2 = (bf16[544,768]{1,0:T(8,128)(2,1)}, bf16[544,768]{1,0:T(8,128)(2,1)}, bf16[544,768]{1,0:T(8,128)(2,1)}, bf16[544,768]{1,0:T(8,128)(2,1)}, f32[16,640]{1,0:T(8,128)}, /*index=5*/bf16[544,768]{1,0:T(8,128)(2,1)}) custom-call(s32[1]{0:T(128)S(6)} %min.10.live_ref, bf16[1024,768]{1,0:T(8,128)(2,1)} %bitcast.7, f32[16,768]{1,0:T(8,128)} %pad.4.mem_ref, ...), custom_call_target="tpu_custom_call" | custom-call | flops 5000000000 | bytes 8000000 | tf_op jit(solution)/shard_map/attn_fwd/pallas_call | solution.py:309
  131.9 19.4 %ffn_fwd.2 = (f32[544,768]{1,0:T(8,128)}, f32[544,1]{1,0:T(8,128)}, bf16[544,768]{1,0:T(8,128)(2,1)}, bf16[544,3072]{1,0:T(8,128)(2,1)}, f32[544,3072]{1,0:T(8,1...) custom-call(s32[1]{0:T(128)S(6)} %min.10.live_ref, ...), custom_call_target="tpu_custom_call" | custom-call | flops 6000000000 | bytes 25000000 | tf_op jit(solution)/shard_map/ffn_fwd/pallas_call | solution.py:330
  151.3 14.3 %attn_fwd.3 = (bf16[544,768]{1,0:T(8,128)(2,1)}, bf16[544,768]{1,0:T(8,128)(2,1)}, bf16[544,768]{1,0:T(8,128)(2,1)}, bf16[544,768]{1,0:T(8,128)(2,1)}, f32[16,640]{1,0:T(8,128)}, /*index=5*/bf16[544,768]{1,0:T(8,128)(2,1)}) custom-call(s32[1]{0:T(128)S(6)} %min.11.live_ref, bf16[1024,768]{1,0:T(8,128)(2,1)} %bitcast.9, f32[16,768]{1,0:T(8,128)} %get-tuple-element.64.mem_ref, ...), custom_call_target="tpu_custom_call" | custom-call | flops 5000000000 | bytes 8000000 | tf_op jit(solution)/shard_map/attn_fwd/pallas_call | solution.py:309
  165.6 19.5 %ffn_fwd.3 = (f32[544,768]{1,0:T(8,128)}, f32[544,1]{1,0:T(8,128)}, bf16[544,768]{1,0:T(8,128)(2,1)}, bf16[544,3072]{1,0:T(8,128)(2,1)}, f32[544,3072]{1,0:T(8,1...) custom-call(s32[1]{0:T(128)S(6)} %min.11.live_ref, ...), custom_call_target="tpu_custom_call" | custom-call | flops 6000000000 | bytes 25000000 | tf_op jit(solution)/shard_map/ffn_fwd/pallas_call | solution.py:330
  185.2 0.6 broadcast_in_dim.24.dmem_ref
  185.8 16.8 %ffn_bwd.2 = (bf16[544,768]{1,0:T(8,128)(2,1)}, bf16[544,3072]{1,0:T(8,128)(2,1)}, bf16[544,768]{1,0:T(8,128)(2,1)}, f32[544,768]{1,0:T(8,128)}, bf16[544,768]{1,0:T(8,128)(2,1)}, /*index=5*/f32[12,768]{1,0:T(8,128)}) custom-call(s32[1]{0:T(128)S(6)} %min.11.live_ref, bf16[1024,768]{1,0:T(8,128)(2,1)} %bitcast.11, f32[16,768]{1,0:T(8,128)} %broadcast_in_dim.24.dmem_ref, ...), custom_call_target="tpu_custom_call" | custom-call | flops 6000000000 | bytes 25000000 | tf_op jit(solution)/shard_map/ffn_bwd/pallas_call | solution.py:356
  202.6 20.7 %attn_bwd.2 = (bf16[544,768]{1,0:T(8,128)(2,1)}, bf16[544,768]{1,0:T(8,128)(2,1)}, bf16[544,768]{1,0:T(8,128)(2,1)}, f32[8,768]{1,0:T(8,128)}, f32[544,768]{1,0:T(8,128)}) custom-call(s32[1]{0:T(128)S(6)} %min.11.live_ref, bf16[544,768]{1,0:T(8,128)(2,1)} %get-tuple-element.70.q_ref, bf16[544,768]{1,0:T(8,128)(2,1)} %get-tuple-element.71.k_ref, ...), custom_call_target="tpu_custom_call" | custom-call | flops 10000000000 | bytes 10000000 | tf_op jit(solution)/shard_map/attn_bwd/pallas_call | solution.py:378
  223.3 1.4 slice_add_fusion.2.dmem_ref
  224.7 16.9 %ffn_bwd.3 = (bf16[544,768]{1,0:T(8,128)(2,1)}, bf16[544,3072]{1,0:T(8,128)(2,1)}, bf16[544,768]{1,0:T(8,128)(2,1)}, f32[544,768]{1,0:T(8,128)}, bf16[544,768]{1,0:T(8,128)(2,1)}, /*index=5*/f32[12,768]{1,0:T(8,128)}) custom-call(s32[1]{0:T(128)S(6)} %min.10.live_ref, bf16[1024,768]{1,0:T(8,128)(2,1)} %bitcast.12, f32[16,768]{1,0:T(8,128)} %slice_add_fusion.2.dmem_ref, ...), custom_call_target="tpu_custom_call" | custom-call | flops 6000000000 | bytes 25000000 | tf_op jit(solution)/shard_map/ffn_bwd/pallas_call | solution.py:356
  241.6 0.0 copy-start.11
  241.6 0.0 copy-start.12
  241.6 0.0 copy-start.8
  241.6 20.4 %attn_bwd.3 = (bf16[544,768]{1,0:T(8,128)(2,1)}, bf16[544,768]{1,0:T(8,128)(2,1)}, bf16[544,768]{1,0:T(8,128)(2,1)}, f32[8,768]{1,0:T(8,128)}, f32[544,768]{1,0:T(8,128)}) custom-call(s32[1]{0:T(128)S(6)} %min.10.live_ref, bf16[544,768]{1,0:T(8,128)(2,1)} %get-tuple-element.67.q_ref, bf16[544,768]{1,0:T(8,128)(2,1)} %get-tuple-element.68.k_ref, ...), custom_call_target="tpu_custom_call" | custom-call | flops 10000000000 | bytes 10000000 | tf_op jit(solution)/shard_map/attn_bwd/pallas_call | solution.py:378
  262.1 0.8 fusion.6
  262.9 0.8 slice_add_fusion.3
  263.7 0.0 copy-done.11
  263.7 0.0 copy-done.12
  263.7 0.6 pad_maximum_fusion.1
  264.3 0.0 copy-done.8
  264.3 0.6 fusion.3
  265.0 0.0 all-reduce.4.cloned.1.call-update
  265.0 0.0 reduce-scatter.2.cloned.1.call-start
  265.0 21.1 %grad_ffn.1 = bf16[6144,768]{1,0:T(8,128)(2,1)} custom-call(bf16[544,3072]{1,0:T(8,128)(2,1)} %get-tuple-element.101.dz0_ref, bf16[544,3072]{1,0:T(8,128)(2,1)} %get-tuple-element.102.dz1_ref, bf16[544,3072]{1,0:T(8,128)(2,1)} %get-tuple-element.103.g0_ref, bf16[544,3072]{1,0:T(8,128)(2,1)} %get-tuple-element.104.g1_ref, ...), custom_call_target="tpu_custom_call" | custom-call | flops 10000000000 | bytes 25000000 | tf_op jit(solution)/shard_map/grad_ffn/pallas_call | solution.py:398
  286.1 13.3 %grad_attn.1 = bf16[3072,768]{1,0:T(8,128)(2,1)} custom-call(bf16[544,768]{1,0:T(8,128)(2,1)} %get-tuple-element.91.x0_ref, bf16[544,768]{1,0:T(8,128)(2,1)} %get-tuple-element.92.x1_ref, bf16[544,768]{1,0:T(8,128)(2,1)} %get-tuple-element.62.a_ref.a0_ref, bf16[544,768]{1,0:T(8,128)(2,1)} %get-tuple-element.65.a_ref.a1_ref, ...), custom_call_target="tpu_custom_call" | custom-call | flops 5000000000 | bytes 15000000 | tf_op jit(solution)/shard_map/grad_attn/pallas_call | solution.py:412
  299.4 16.9 %pad_maximum_fusion = bf16[9216,768]{1,0:T(8,128)(2,1)} fusion(bf16[6144,768]{1,0:T(8,128)(2,1)} %grad_ffn.1, bf16[3072,768]{1,0:T(8,128)(2,1)} %grad_attn.1), kind=kLoop, calls=%fused_computation | loop fusion | flops 28311552 | bytes 28311552 | tf_op jit(solution)/shard_map/concatenate | solution.py:472
  316.3 0.0 reduce-scatter.2.cloned.1.call-update
  316.4 1.4 copy-done.3
  317.8 0.1 slice.29
  317.9 1.3 copy-done.2
  319.2 0.1 slice.30
  319.3 0.4 copy-done.4
  319.7 0.5 copy-done.5
  320.2 0.0 copy-start.6
  320.2 0.0 copy-start.7
  320.2 3.1 maximum_bitcast_fusion
  323.3 61.1 %all-reduce.4.cloned.1.call-done = (f32[10,768]{1,0:T(8,128)}, f32[12,768]{1,0:T(8,128)}) async-done(((f32[10,768]{1,0:T(8,128)}, f32[12,768]{1,0:T(8,128)}), (f32[10,768]{1,0:T(8,128)}, f32[12,768]{1,0:T(8,128)})) %all-reduce.4.cloned.1.call-update) | async-done | bytes 67600 | tf_op jit(solution)/shard_map/psum | solution.py:474
  384.4 1.4 broadcast_multiply_fusion.1
  385.8 0.0 copy-done.1
  385.9 1.5 multiply_add_fusion.1
  387.3 166.9 %reduce-scatter.2.cloned.1.call-done = bf16[288,768]{1,0:T(8,128)(2,1)} async-done(((bf16[9216,768]{1,0:T(8,128)(2,1)}), bf16[288,768]{1,0:T(8,128)(2,1)}) %reduce-scatter.2.cloned.1.call-update) | async-done | bytes 442384 | tf_op jit(solution)/shard_map/reduce_scatter | solution.py:473
  554.2 0.0 copy-done.6
  554.2 3.3 multiply_add_fusion
  (13 shorter events, 0.0 us)
Async XLA Ops:
  7.2 110.4 %all-gather.2.cloned.1.call-start = ((), (), s32[]{:S(2)}) async-start(), calls=%async_computation.1 | async-start | bytes 14598144 | tf_op jit(solution)/shard_map/all_gather | solution.py:469
  9.2 375.2 %all-reduce.4.cloned.1.call-start = ((), (), s32[]{:S(2)}) async-start(), calls=%async_computation.3 | async-start | bytes 196608 | tf_op jit(solution)/shard_map/psum | solution.py:474
  241.6 22.1 %copy-start.11 = (f32[12,768]{1,0:T(8,128)S(1)}, f32[12,768]{1,0:T(8,128)}, u32[]{:S(2)}) copy-start(f32[12,768]{1,0:T(8,128)} %get-tuple-element.112) | copy-start | bytes 110596
  241.6 22.1 %copy-start.12 = (f32[12,768]{1,0:T(8,128)S(1)}, f32[12,768]{1,0:T(8,128)}, u32[]{:S(2)}) copy-start(f32[12,768]{1,0:T(8,128)} %get-tuple-element.111) | copy-start | bytes 110596
  241.6 22.7 %copy-start.8 = (f32[16,768]{1,0:T(8,128)S(1)}, f32[16,768]{1,0:T(8,128)}, u32[]{:S(2)}) copy-start(f32[16,768]{1,0:T(8,128)} %slice_add_fusion.2.dmem_ref) | copy-start | bytes 147460
  265.0 289.2 %reduce-scatter.2.cloned.1.call-start = ((), (), s32[]{:S(2)}) async-start(), calls=%async_computation.2 | async-start | bytes 14598144 | tf_op jit(solution)/shard_map/reduce_scatter | solution.py:473
  316.3 1.4 copy-start.3
  317.8 1.4 copy-start.2
  317.8 1.9 copy-start.4
  317.8 2.4 copy-start.5
  320.2 65.7 %copy-start.1 = (f32[12,768]{1,0:T(8,128)S(1)}, f32[12,768]{1,0:T(8,128)}, u32[]{:S(2)}) copy-start(f32[12,768]{1,0:T(8,128)} %vec_ref.11) | copy-start | bytes 110596
  320.2 65.7 %copy-start.9 = (f32[12,768]{1,0:T(8,128)S(1)}, f32[12,768]{1,0:T(8,128)}, u32[]{:S(2)}) copy-start(f32[12,768]{1,0:T(8,128)} %param.18) | copy-start | bytes 110596
  320.2 65.7 %copy-start.10 = (f32[12,768]{1,0:T(8,128)S(1)}, f32[12,768]{1,0:T(8,128)}, u32[]{:S(2)}) copy-start(f32[12,768]{1,0:T(8,128)} %param.19) | copy-start | bytes 110596
  320.2 234.1 %copy-start = (f32[288,768]{1,0:T(8,128)S(1)}, f32[288,768]{1,0:T(8,128)}, u32[]{:S(2)}) copy-start(f32[288,768]{1,0:T(8,128)} %param.14) | copy-start | bytes 2654212
  320.2 234.1 %copy-start.6 = (f32[288,768]{1,0:T(8,128)S(1)}, f32[288,768]{1,0:T(8,128)}, u32[]{:S(2)}) copy-start(f32[288,768]{1,0:T(8,128)} %param.15) | copy-start | bytes 2654212
  320.2 234.0 %copy-start.7 = (f32[288,768]{1,0:T(8,128)S(1)}, f32[288,768]{1,0:T(8,128)}, u32[]{:S(2)}) copy-start(f32[288,768]{1,0:T(8,128)} %param.16) | copy-start | bytes 2654212
Sparse Core Ops, SparseCore 0:
  11.6 105.9 all-gather.1
  265.1 119.2 all-reduce.3
  390.4 163.7 reduce-scatter.1
